TPU v7x, 32 devices: a whole 2x2x4 slice. The times are simulated.
32 devices in a mesh: tau: 2 (over x), row: 16 (over z, y, core).
Axes of the slice: x: 2, y: 2, z: 4, core: 2. Of those that a mesh axis runs over, the one named last changes fastest.
Arguments:
- integrals: bfloat16 [2048, 3, 3, 4096], P('row'), may hold values from -0.3125 to 0.3125
- occupied: bfloat16 [32, 3, 64, 64], P('tau'), parts along dimension 0, may hold values from -0.4375 to 0.4375
- virtual: bfloat16 [32, 3, 64, 64], P('tau'), parts along dimension 0, may hold values from -0.4375 to 0.4375
- tile_mask: int32 [16, 3, 3], replicated, may hold values 0 or 1
Outputs:
- response: float32 [4096, 640], P(('tau', 'row')), parts along dimension 0
There are 2 independent parts, one for each index of `tau`. A program takes and returns all parts, laid end to end along the dimension named above; an argument that names none is the same for every part. Nothing has to cross between parts.
All inputs are finite; a program needn't handle non-finite values.
Results may differ from a plain program's by a relative error of at most 0.0041.
Values may be sent and summed in bfloat16 or wider, within the bound.
A program may use at most 128 MiB of HBM per device.

v0:
```python
import jax
import jax.numpy as jnp
from jax import lax
from jax.sharding import PartitionSpec as P


def shifted(value, axis, steps):
    count = lax.axis_size(axis)
    pairs = [(source, (source + steps) % count) for source in range(count)]
    return lax.ppermute(value, axis, pairs)


def occupied_side(masked, occ_near, column):
    col_count = masked.shape[1]
    band_count = masked.shape[2]
    middle = band_count // 2
    row_tiles = []
    for band in range(band_count):
        summed = None
        for inner in range(col_count):
            offset = column - inner + band
            second = column - inner + middle
            if 0 <= offset < band_count and 0 <= second < band_count:
                term = jnp.einsum(
                    "puv,vl->pul",
                    masked[:, inner, offset],
                    occ_near[inner, second],
                    preferred_element_type=jnp.float32,
                )
                summed = term if summed is None else summed + term
        row_tiles.append(summed.astype(jnp.bfloat16))
    return row_tiles


def virtual_side(product_tiles, vir_column):
    band_count = len(product_tiles)
    middle = band_count // 2
    row_tiles = []
    for sigma in range(band_count):
        summed = None
        for band in range(band_count):
            second = band - sigma + middle
            if 0 <= second < band_count:
                term = jnp.einsum(
                    "su,pul->psl",
                    vir_column[sigma, second],
                    product_tiles[band],
                    preferred_element_type=jnp.float32,
                )
                summed = term if summed is None else summed + term
        row_tiles.append(summed.astype(jnp.bfloat16))
    return row_tiles


def per_device(integrals, occupied, virtual, tile_mask):
    ri_rows, col_count, band_count, square = integrals.shape
    width = occupied.shape[-1]
    blocks = occupied.shape[0]
    reach = col_count // 2
    middle = band_count // 2
    position = lax.axis_index("row")
    gate = lax.dynamic_index_in_dim(tile_mask, position, 0, keepdims=False)
    masked = (integrals * gate[None, :, :, None].astype(jnp.bfloat16)).reshape(
        ri_rows, col_count, band_count, width, width
    )
    occ_near = jnp.take(
        occupied, (position - reach + jnp.arange(col_count, dtype=jnp.int32)) % blocks, axis=0
    )
    own_virtual = jnp.take(
        virtual, (position - middle + jnp.arange(band_count, dtype=jnp.int32)) % blocks, axis=0
    )
    virt_rows = []
    partner_rows = []
    moved_masked = []
    for column in reversed(range(col_count)):
        slab = masked[:, column]
        if column != reach:
            slab = shifted(slab, "row", column - reach)
        moved_masked.append(slab)
    for index in range(col_count):
        column = col_count - 1 - index
        slab = jnp.stack(occupied_side(masked, occ_near, column), axis=1)
        if column != reach:
            slab = shifted(slab, "row", column - reach)
        tiles = [slab[:, band] for band in range(band_count)]
        virt_rows.append(jnp.stack(virtual_side(tiles, own_virtual), axis=1))
        partner_rows.append(moved_masked[index])
    flat_virtual = jnp.concatenate(virt_rows, axis=0).reshape(col_count * ri_rows, -1)
    flat_partner = jnp.concatenate(partner_rows, axis=0).reshape(col_count * ri_rows, -1)
    partial_value = lax.dot_general(
        flat_virtual, flat_partner, (((1,), (1,)), ((), ())), preferred_element_type=jnp.float32
    )
    total = jnp.zeros((ri_rows, (2 * col_count - 1) * ri_rows), jnp.float32)
    for index in range(col_count):
        offset = index - reach
        slab = partial_value[index * ri_rows : (index + 1) * ri_rows]
        if offset != 0:
            slab = shifted(slab, "row", offset)
        total = total + jnp.pad(
            slab, ((0, 0), ((reach - offset) * ri_rows, (reach + offset) * ri_rows))
        )
    return -2.0 * total


def solution(mesh):
    in_specs = (
        P("row", None, None, None),
        P("tau", None, None, None),
        P("tau", None, None, None),
        P(),
    )
    out_specs = P(("tau", "row"), None)
    return jax.shard_map(
        per_device, mesh=mesh, in_specs=in_specs, out_specs=out_specs, check_vma=False
    )
```

profile of v0, /device:TPU:0, one launch (start us, length us, event | category | flops | bytes accessed | tf_op | source)
XLA Modules:
  0.0 195.0 jit_solution(1303339143752366649)
XLA Ops:
  0.0 0.9 fusion.86
  1.0 8.0 %broadcast_multiply_fusion = bf16[128,3,3,4096]{3,0,2,1:T(8,128)(2,1)} fusion(bf16[128,3,3,4096]{3,0,2,1:T(8,128)(2,1)} %param.6, bf16[3,3]{1,0:T(4,128)(2,1)S(1)} %fusion.86), kind=kLoop, calls=%fused_computation.22 | loop fusion | flops 4718592 | bytes 18874386 | tf_op jit(solution)/shard_map/mul | solution.py:63
  9.0 12.7 %copy.28 = bf16[128,3,3,4096]{0,3,2,1:T(8,128)(2,1)} copy(bf16[128,3,3,4096]{3,0,2,1:T(8,128)(2,1)} %broadcast_multiply_fusion) | data formatting | bytes 18874368 | tf_op jit(solution)/shard_map/mul | solution.py:63
  22.5 1.6 fusion.69
  24.1 1.8 fusion.39
  25.9 2.0 %fusion.19 = bf16[128,1,64,64]{0,3,2,1:T(8,128)(2,1)S(1)} fusion(bf16[128,3,3,64,64]{0,4,3,2,1:T(8,128)(2,1)} %bitcast.202, bf16[3,3,64,64]{2,3,1,0:T(8,128)(2,1)S(1)} %broadcast_select_fusion.1), kind=kOutput, calls=%fused_computation.46 | convolution fusion | flops 67633152 | bytes 2113536 | tf_op jit(solution)/shard_map/puv,vl->pul/dot_general | solution.py:24
  28.0 1.6 fusion.21
  30.1 2.0 %pad_maximum_fusion.1 = bf16[128,3,64,64]{0,3,2,1:T(8,128)(2,1)} fusion(bf16[128,1,64,64]{0,3,2,1:T(8,128)(2,1)S(1)} %fusion.19, bf16[128,1,64,64]{0,3,2,1:T(8,128)(2,1)S(1)} %fusion.22, bf16[128,1,64,64]{0,3,2,1:T(8,128)(2,1)S(1)} %fusion.21), kind=kLoop, calls=%fused_computation.26 | loop fusion | flops 3145728 | bytes 6291456 | tf_op jit(solution)/shard_map/stack | solution.py:82
  34.5 2.0 %pad_maximum_fusion.2 = bf16[128,3,64,64]{0,3,2,1:T(8,128)(2,1)} fusion(bf16[128,1,64,64]{0,3,2,1:T(8,128)(2,1)S(1)} %fusion.29, bf16[128,1,64,64]{0,3,2,1:T(8,128)(2,1)S(1)} %fusion.28, bf16[128,1,64,64]{0,3,2,1:T(8,128)(2,1)S(1)} %fusion.20), kind=kLoop, calls=%fused_computation.27 | loop fusion | flops 3145728 | bytes 6291456 | tf_op jit(solution)/shard_map/stack | solution.py:82
  36.6 5.0 %collective-permute-start.1 = (bf16[128,3,64,64]{0,3,2,1:T(8,128)(2,1)}, bf16[128,3,64,64]{0,3,2,1:T(8,128)(2,1)}, u32[]{:S(2)}, u32[]{:S(2)}) collective-permute-start(bf16[128,3,64,64]{0,3,2,1:T(8,128)(2,1)} %pad_maximum_fusion.2), channel_id=1, source_target_pairs={{0,15},{1,0},{2,1},{3,2},{4,3},{5,4},{6,5},{7,6},{8,7},{9,8},{10,9... | collective-permute-start | bytes 9437192 | tf_op jit(solution)/shard_map/ppermute | solution.py:10
  41.6 4.7 %slice_bitcast_fusion.2 = (bf16[128,3,64,64]{0,3,2,1:T(8,128)(2,1)}, bf16[128,3,64,64]{0,3,2,1:T(8,128)(2,1)}, bf16[128,3,64,64]{0,3,2,1:T(8,128)(2,1)}) fusion(bf16[128,3,3,64,64]{0,4,3,2,1:T(8,128)(2,1)S(1)} %bitcast.213), kind=kLoop, calls=%fused_computation.25 | loop fusion | bytes 18874368 | tf_op jit(solution)/shard_map/squeeze | solution.py:76
  46.3 4.4 %collective-permute-start.3 = (bf16[128,3,64,64]{0,3,2,1:T(8,128)(2,1)}, bf16[128,3,64,64]{0,3,2,1:T(8,128)(2,1)}, u32[]{:S(2)}, u32[]{:S(2)}) collective-permute-start(bf16[128,3,64,64]{0,3,2,1:T(8,128)(2,1)} %get-tuple-element.7), channel_id=1, source_target_pairs={{0,15},{1,0},{2,1},{3,2},{4,3},{5,4},{6,5},{7,6},{8,7},{9,8},{10,9... | collective-permute-start | bytes 9437192 | tf_op jit(solution)/shard_map/ppermute | solution.py:10
  51.2 1.7 fusion.70
  52.9 1.8 fusion.41
  54.7 1.7 fusion.40
  56.4 1.7 gather_fusion.1
  58.2 2.5 %add_convert_fusion.10 = bf16[128,64,64]{0,2,1:T(8,128)(2,1)S(1)} fusion(f32[128,64,64]{0,2,1:T(8,128)} %fusion.41, bf16[128,3,3,64,64]{0,4,3,2,1:T(8,128)(2,1)} %bitcast.204, bf16[3,3,64,64]{2,3,1,0:T(8,128)(2,1)S(1)} %broadcast_select_fusion.1), kind=kOutput, calls=%fused_computation.38 | convolution fusion | flops 68157440 | bytes 4210688 | tf_op jit(solution)/shard_map/puv,vl->pul/dot_general | solution.py:24
  61.6 1.7 add_convert_fusion.9
  63.3 1.0 fusion.25
  64.3 0.9 fusion.79
  65.2 1.6 add_convert_fusion.7
  66.9 1.0 fusion.27
  67.9 0.9 fusion.77
  68.8 0.9 fusion.58
  69.7 1.1 fusion.26
  70.8 2.0 %collective-permute-done = bf16[128,3,64,64]{0,3,2,1:T(8,128)(2,1)} collective-permute-done((bf16[128,3,64,64]{0,3,2,1:T(8,128)(2,1)}, bf16[128,3,64,64]{0,3,2,1:T(8,128)(2,1)}, u32[]{:S(2)}, u32[]{:S(2)}) %collective-permute-start) | collective-permute-done | bytes 3145760 | tf_op jit(solution)/shard_map/ppermute | solution.py:10
  72.8 2.5 %slice_bitcast_fusion.13 = (bf16[128,64,64]{0,2,1:T(8,128)(2,1)S(1)}, bf16[128,64,64]{0,2,1:T(8,128)(2,1)S(1)}, bf16[128,64,64]{0,2,1:T(8,128)(2,1)S(1)}) fusion(bf16[128,3,64,64]{0,3,2,1:T(8,128)(2,1)} %collective-permute-done), kind=kLoop, calls=%fused_computation.71 | loop fusion | bytes 6291456 | tf_op jit(solution)/shard_map/squeeze | solution.py:85
  76.3 1.0 fusion.24
  77.3 0.9 fusion.81
  78.2 2.5 %slice_bitcast_fusion.5 = (bf16[128,64,64]{0,2,1:T(8,128)(2,1)S(1)}, bf16[128,64,64]{0,2,1:T(8,128)(2,1)S(1)}, bf16[128,64,64]{0,2,1:T(8,128)(2,1)S(1)}) fusion(bf16[128,3,64,64]{0,3,2,1:T(8,128)(2,1)} %collective-permute-done.1), kind=kLoop, calls=%fused_computation.64 | loop fusion | bytes 6291456 | tf_op jit(solution)/shard_map/squeeze | solution.py:85
  80.7 1.2 fusion.23
  81.9 0.9 fusion.47
  82.8 1.0 fusion.31
  83.8 0.9 fusion.71
  84.7 1.0 fusion.30
  85.7 0.9 fusion.67
  86.6 0.9 fusion.83
  87.6 0.9 fusion.52
  88.5 0.9 fusion.73
  89.4 1.1 fusion.37
  90.5 1.1 fusion.38
  91.6 14.9 %collective-permute-done.2 = bf16[128,3,64,64]{0,3,2,1:T(8,128)(2,1)} collective-permute-done((bf16[128,3,64,64]{0,3,2,1:T(8,128)(2,1)}, bf16[128,3,64,64]{0,3,2,1:T(8,128)(2,1)}, u32[]{:S(2)}, u32[]{:S(2)}) %collective-permute-start.2) | collective-permute-done | bytes 3145760 | tf_op jit(solution)/shard_map/ppermute | solution.py:10
  106.5 3.9 %collective-permute-done.3 = bf16[128,3,64,64]{0,3,2,1:T(8,128)(2,1)} collective-permute-done((bf16[128,3,64,64]{0,3,2,1:T(8,128)(2,1)}, bf16[128,3,64,64]{0,3,2,1:T(8,128)(2,1)}, u32[]{:S(2)}, u32[]{:S(2)}) %collective-permute-start.3) | collective-permute-done | bytes 3145760 | tf_op jit(solution)/shard_map/ppermute | solution.py:10
  110.4 4.9 %pad_maximum_fusion = bf16[384,3,64,64]{0,3,2,1:T(8,128)(2,1)S(1)} fusion(bf16[128,3,64,64]{0,3,2,1:T(8,128)(2,1)} %collective-permute-done.3, bf16[128,3,64,64]{0,3,2,1:T(8,128)(2,1)S(1)} %copy-done.3, bf16[128,3,64,64]{0,3,2,1:T(8,128)(2,1)} %collective-permute-done.2), kind=kLoop, calls=%fused_computation.20 | loop fusion | flops 28311552 | bytes 18874368 | tf_op jit(solution)/shard_map/concatenate | solution.py:89
  115.3 7.2 %fusion.32 = f32[384,384]{1,0:T(8,128)S(1)} fusion(bf16[384,3,64,64]{0,3,2,1:T(8,128)(2,1)S(1)} %pad_maximum_fusion, bf16[128,1,64,64]{0,2,3,1:T(8,128)(2,1)S(1)} %fusion.31, bf16[128,1,64,64]{0,2,3,1:T(8,128)(2,1)S(1)} %fusion.38, bf16[128,1,64,64]{0,2,3,1:T(8,128)(2,1)S(1)} %fusion.30, bf16[128,1,64,64]{0,2,3,1:T(8,128)(2,1)S(1)} %fusion.27, ...), kind=kOutput, calls=%fused_computation.59 | convolution fusion | flops 3708813312 | bytes 19464192 | tf_op jit(solution)/shard_map/dot_general | solution.py:90
  122.6 4.8 %collective-permute-start.4 = (f32[128,384]{1,0:T(8,128)S(1)}, f32[128,384]{1,0:T(8,128)S(1)}, u32[]{:S(2)}, u32[]{:S(2)}) collective-permute-start(f32[128,384]{1,0:T(8,128)S(1)} %get-tuple-element.15), channel_id=1, source_target_pairs={{0,15},{1,0},{2,1},{3,2},{4,3},{5,4},{6,5},{7,6},{8,7},{9,8},{10,9... | collective-permute-start | bytes 589832 | tf_op jit(solution)/shard_map/ppermute | solution.py:10
  127.4 58.6 %collective-permute-start.5 = (f32[128,384]{1,0:T(8,128)S(1)}, f32[128,384]{1,0:T(8,128)S(1)}, u32[]{:S(2)}, u32[]{:S(2)}) collective-permute-start(f32[128,384]{1,0:T(8,128)S(1)} %get-tuple-element.16), channel_id=1, source_target_pairs={{0,1},{1,2},{2,3},{3,4},{4,5},{5,6},{6,7},{7,8},{8,9},{9,10},{10,1... | collective-permute-start | bytes 589832 | tf_op jit(solution)/shard_map/ppermute | solution.py:10
  186.8 7.4 %collective-permute-done.5 = f32[128,384]{1,0:T(8,128)S(1)} collective-permute-done((f32[128,384]{1,0:T(8,128)S(1)}, f32[128,384]{1,0:T(8,128)S(1)}, u32[]{:S(2)}, u32[]{:S(2)}) %collective-permute-start.5) | collective-permute-done | bytes 196640 | tf_op jit(solution)/shard_map/ppermute | solution.py:10
  (34 shorter events, 7.7 us)
Async XLA Ops:
  0.0 21.6 %copy-start = (bf16[16,3,64,64]{3,2,1,0:T(8,128)(2,1)S(1)}, bf16[16,3,64,64]{3,2,1,0:T(8,128)(2,1)}, u32[]{:S(2)}) copy-start(bf16[16,3,64,64]{3,2,1,0:T(8,128)(2,1)} %param.7) | copy-start | bytes 1179652
  24.1 5.5 %copy-start.2 = (bf16[128,3,3,4096]{0,3,2,1:T(8,128)(2,1)S(1)}, bf16[128,3,3,4096]{0,3,2,1:T(8,128)(2,1)}, u32[]{:S(2)}) copy-start(bf16[128,3,3,4096]{0,3,2,1:T(8,128)(2,1)} %copy.28) | copy-start | bytes 28311556
  32.0 40.8 %collective-permute-start = (bf16[128,3,64,64]{0,3,2,1:T(8,128)(2,1)}, bf16[128,3,64,64]{0,3,2,1:T(8,128)(2,1)}, u32[]{:S(2)}, u32[]{:S(2)}) collective-permute-start(bf16[128,3,64,64]{0,3,2,1:T(8,128)(2,1)} %pad_maximum_fusion.1), channel_id=1, source_target_pairs={{0,1},{1,2},{2,3},{3,4},{4,5},{5,6},{6,7},{7,8},{8,9},{9,10},{10,1... | collective-permute-start | bytes 9437192 | tf_op jit(solution)/shard_map/ppermute | solution.py:10
  36.6 41.6 %collective-permute-start.1 = (bf16[128,3,64,64]{0,3,2,1:T(8,128)(2,1)}, bf16[128,3,64,64]{0,3,2,1:T(8,128)(2,1)}, u32[]{:S(2)}, u32[]{:S(2)}) collective-permute-start(bf16[128,3,64,64]{0,3,2,1:T(8,128)(2,1)} %pad_maximum_fusion.2), channel_id=1, source_target_pairs={{0,15},{1,0},{2,1},{3,2},{4,3},{5,4},{6,5},{7,6},{8,7},{9,8},{10,9... | collective-permute-start | bytes 9437192 | tf_op jit(solution)/shard_map/ppermute | solution.py:10
  46.3 60.2 %collective-permute-start.2 = (bf16[128,3,64,64]{0,3,2,1:T(8,128)(2,1)}, bf16[128,3,64,64]{0,3,2,1:T(8,128)(2,1)}, u32[]{:S(2)}, u32[]{:S(2)}) collective-permute-start(bf16[128,3,64,64]{0,3,2,1:T(8,128)(2,1)} %get-tuple-element.6), channel_id=1, source_target_pairs={{0,1},{1,2},{2,3},{3,4},{4,5},{5,6},{6,7},{7,8},{8,9},{9,10},{10,1... | collective-permute-start | bytes 9437192 | tf_op jit(solution)/shard_map/ppermute | solution.py:10
  46.3 64.1 %collective-permute-start.3 = (bf16[128,3,64,64]{0,3,2,1:T(8,128)(2,1)}, bf16[128,3,64,64]{0,3,2,1:T(8,128)(2,1)}, u32[]{:S(2)}, u32[]{:S(2)}) collective-permute-start(bf16[128,3,64,64]{0,3,2,1:T(8,128)(2,1)} %get-tuple-element.7), channel_id=1, source_target_pairs={{0,15},{1,0},{2,1},{3,2},{4,3},{5,4},{6,5},{7,6},{8,7},{9,8},{10,9... | collective-permute-start | bytes 9437192 | tf_op jit(solution)/shard_map/ppermute | solution.py:10
  58.2 3.4 %copy-start.4 = (f32[128,64,64]{0,2,1:T(8,128)S(1)}, f32[128,64,64]{0,2,1:T(8,128)}, u32[]{:S(2)}) copy-start(f32[128,64,64]{0,2,1:T(8,128)} %fusion.70) | copy-start | bytes 6291460
  63.3 1.9 copy-start.5
  90.5 19.9 %copy-start.3 = (bf16[128,3,64,64]{0,3,2,1:T(8,128)(2,1)S(1)}, bf16[128,3,64,64]{0,3,2,1:T(8,128)(2,1)}, u32[]{:S(2)}) copy-start(bf16[128,3,64,64]{0,3,2,1:T(8,128)(2,1)} %get-tuple-element.8) | copy-start | bytes 9437188
  115.3 79.7 %copy-start.1 = (bf16[16,3,64,64]{3,2,1,0:T(8,128)(2,1)S(1)}, bf16[16,3,64,64]{3,2,1,0:T(8,128)(2,1)}, u32[]{:S(2)}) copy-start(bf16[16,3,64,64]{3,2,1,0:T(8,128)(2,1)} %param.7) | copy-start | bytes 1179652
  122.6 64.2 %collective-permute-start.4 = (f32[128,384]{1,0:T(8,128)S(1)}, f32[128,384]{1,0:T(8,128)S(1)}, u32[]{:S(2)}, u32[]{:S(2)}) collective-permute-start(f32[128,384]{1,0:T(8,128)S(1)} %get-tuple-element.15), channel_id=1, source_target_pairs={{0,15},{1,0},{2,1},{3,2},{4,3},{5,4},{6,5},{7,6},{8,7},{9,8},{10,9... | collective-permute-start | bytes 589832 | tf_op jit(solution)/shard_map/ppermute | solution.py:10
  127.4 66.9 %collective-permute-start.5 = (f32[128,384]{1,0:T(8,128)S(1)}, f32[128,384]{1,0:T(8,128)S(1)}, u32[]{:S(2)}, u32[]{:S(2)}) collective-permute-start(f32[128,384]{1,0:T(8,128)S(1)} %get-tuple-element.16), channel_id=1, source_target_pairs={{0,1},{1,2},{2,3},{3,4},{4,5},{5,6},{6,7},{7,8},{8,9},{9,10},{10,1... | collective-permute-start | bytes 589832 | tf_op jit(solution)/shard_map/ppermute | solution.py:10
where the time goes:
time: 196 us; the launch traced here: 195 us
  starting transfers between devices  73.2 us (37%)
  matrix products  48.7 us (25%)
  waiting for transfers between devices  29.1 us (15%)
  local copies, waits for them, and re-layouts  25 us (13%)
  other arithmetic  18.8 us (10%)
    ppermute x6, starting transfers between devices, shifted(): return lax.ppermute(value, axis, pairs)  73.2 us
    ppermute x6, waiting for transfers between devices, shifted(): return lax.ppermute(value, axis, pairs)  29.1 us
    dot_general x17, matrix products, occupied_side(): jnp.einsum('puv,vl->pul', masked[:, inner, offset], occ_near[inner, secon...  21.1 us
    dot_general x21, matrix products, virtual_side(): jnp.einsum('su,pul->psl', vir_column[sigma, second], product_tiles[band],...  20.4 us
    mul x1, local copies, waits for them, and re-layouts, per_device(): integrals * gate[None, :, :, None].astype(jnp.bfloat16)  12.7 us
    mul x1, other arithmetic, per_device(): integrals * gate[None, :, :, None].astype(jnp.bfloat16)  8 us
    dot_general x1, matrix products, per_device(): lax.dot_general(flat_virtual, flat_partner, (((1,), (1,)), ((), ())), pre...  7.24 us
    squeeze x2, local copies, waits for them, and re-layouts, per_device(): tiles = [slab[:, band] for band in range(band_count)]  5.09 us
  transfers between devices with their start and end apart: 6, of which 5 were waited for; matrix products, arithmetic and copies ran while one was open for 24% of the time, Pallas kernels for 0%

commit v1 on v0

v1 whole, which is shorter than its diff:
```python
import functools

import jax
import jax.numpy as jnp
from jax import lax
from jax.experimental import pallas as pl
from jax.experimental.pallas import tpu as pltpu
from jax.sharding import PartitionSpec as P

F32 = jnp.float32
BF16 = jnp.bfloat16
MESH = pl.DeviceIdType.MESH
NB_TILES = 5
OWN_TERMS = (((0, 1), (1, 3)), ((0, 2), (1, 4), (2, 6)), ((1, 5), (2, 7)))


def kernel(
    tau_count, row_count, width,
    tiles_ref, weight_ref, virt_ref, gate_ref,
    out_ref,
    own, near, prod, part, virt, panels, sending, arriving, total,
    own_sem, inner_send, inner_recv, outer_send, outer_recv, fwd_send, fwd_recv, end_send, end_recv,
):
    rows = own.shape[1]
    square = own.shape[2]
    tau = lax.axis_index("tau")
    me = lax.axis_index("row")
    odd = lax.rem(me, 2)
    inner = me + 1 - 2 * odd
    outer = lax.rem(me - 1 + 2 * odd + row_count, row_count)
    share = rows // tau_count
    first = pl.multiple_of(tau * share, share)

    barrier = pltpu.get_barrier_semaphore()
    pl.semaphore_signal(barrier, inc=1, device_id={"row": inner}, device_id_type=MESH)
    pl.semaphore_signal(barrier, inc=1, device_id={"row": outer}, device_id_type=MESH)
    for step in range(1, tau_count):
        pl.semaphore_signal(
            barrier, inc=1, device_id={"tau": lax.rem(tau + step, tau_count)}, device_id_type=MESH
        )
    pl.semaphore_wait(barrier, tau_count + 1)

    outer_copies = []
    for t in range(NB_TILES):
        copy = pltpu.make_async_remote_copy(
            src_ref=tiles_ref.at[4 * odd + t, pl.ds(first, share)],
            dst_ref=near.at[1, t, pl.ds(first, share)],
            send_sem=outer_send.at[t], recv_sem=outer_recv.at[t],
            device_id={"row": outer}, device_id_type=MESH,
        )
        copy.start()
        outer_copies.append(copy)
    own_copy = pltpu.make_async_copy(tiles_ref, own, own_sem)
    own_copy.start()
    inner_copies = []
    for t in range(NB_TILES):
        copy = pltpu.make_async_remote_copy(
            src_ref=tiles_ref.at[4 * (1 - odd) + t],
            dst_ref=near.at[0, t],
            send_sem=inner_send.at[t], recv_sem=inner_recv.at[t],
            device_id={"row": inner}, device_id_type=MESH,
        )
        copy.start()
        inner_copies.append(copy)

    fwd_copies = []

    def forward(t):
        outer_copies[t].wait_recv()
        for step in range(1, tau_count):
            place = near.at[1, t, pl.ds(first, share)]
            copy = pltpu.make_async_remote_copy(
                src_ref=place, dst_ref=place,
                send_sem=fwd_send.at[t, step - 1], recv_sem=fwd_recv.at[t, step - 1],
                device_id={"tau": lax.rem(tau + step, tau_count)}, device_id_type=MESH,
            )
            copy.start()
            fwd_copies.append(copy)

    def products(load, base, terms):
        def at(step, carry):
            lane = pl.multiple_of(step * 256, 256)
            for o in range(3):
                halves = []
                for half in range(2):
                    halves.append(jnp.concatenate(
                        [load(t, pl.ds(lane + 128 * half, 128)) for unused, t in terms[o]], axis=1))
                weight = jnp.concatenate([weight_ref[base + k, o] for k, unused in terms[o]], axis=1)
                result = lax.dot_general(
                    weight, jnp.concatenate(halves, axis=0), (((1,), (1,)), ((), ())),
                    preferred_element_type=F32)
                prod[o, pl.ds(lane, 128), :] = result[:, :rows]
                prod[o, pl.ds(lane + 128, 128), :] = result[:, rows:]
            return carry

        lax.fori_loop(0, square // 256, at, 0)

    def virtual(block):
        def at(step, carry):
            columns = []
            for half in range(2):
                columns.append(jnp.concatenate(
                    [prod[m, pl.ds(2 * step + half, width, stride=width), :] for m in range(3)], axis=0))
            right = jnp.concatenate(columns, axis=1).astype(BF16)
            result = jnp.dot(virt_ref[...], right, preferred_element_type=F32)
            for half in range(2):
                for m in range(3):
                    part[m, pl.ds(2 * step + half, width, stride=width), :] = result[
                        m * width:(m + 1) * width, half * rows:(half + 1) * rows]
            return carry

        lax.fori_loop(0, width // 2, at, 0)

        def rounded(step, carry):
            place = pl.ds(pl.multiple_of(step * 512, 512), 512)
            for m in range(3):
                virt[m, place, block * rows:(block + 1) * rows] = part[m, place, :].astype(BF16)
            return carry

        lax.fori_loop(0, square // 512, rounded, 0)

    def panel(load, slot, low, high):
        result = None
        for m in range(3):
            def at(step, carry, m=m):
                place = pl.ds(pl.multiple_of(step * 512, 512), 512)
                return carry + jnp.dot(
                    load(m, place), virt[m, place, low * rows:high * rows],
                    preferred_element_type=F32)

            term = lax.fori_loop(
                0, square // 512, at, jnp.zeros((rows, (high - low) * rows), F32))
            term = term * gate_ref[slot, m]
            result = term if result is None else result + term
        panels[slot, :, low * rows:high * rows] = result

    def near_load(slot):
        return lambda t, lanes: near[slot, t, :, lanes]

    def near_partner(slot, offset):
        return lambda m, lanes: near[slot, offset + m, :, lanes]

    def own_load(t, lanes):
        return own[t, :, lanes]

    def own_partner(m, lanes):
        return own[3 + m, :, lanes]

    near_terms = tuple(((0, o), (1, 2 + o)) for o in range(3))

    own_copy.wait()
    products(own_load, 0, OWN_TERMS)
    virtual(0)
    forward(0)
    panel(own_partner, 0, 0, 1)
    for copy in inner_copies:
        copy.wait_recv()
    products(near_load(0), 3, near_terms)
    forward(1)
    virtual(1)
    panel(near_partner(0, 2 * odd), 1, 0, 2)
    panel(own_partner, 0, 1, 2)
    for t in range(2, NB_TILES):
        forward(t)
    for copy in fwd_copies:
        copy.wait_recv()
    products(near_load(1), 5, near_terms)
    virtual(2)
    panel(near_partner(1, 2 * (1 - odd)), 2, 0, 3)
    panel(own_partner, 0, 2, 3)
    panel(near_partner(0, 2 * odd), 1, 2, 3)

    places = (1, 2 * (1 - odd), 2 * odd)
    for block in (1, 2):
        for slot in range(3):
            sending[block - 1, places[slot]] = panels[slot, :, block * rows:(block + 1) * rows].T
    end_copies = []
    for block, target in ((1, inner), (2, outer)):
        copy = pltpu.make_async_remote_copy(
            src_ref=sending.at[block - 1], dst_ref=arriving.at[block - 1],
            send_sem=end_send.at[block - 1], recv_sem=end_recv.at[block - 1],
            device_id={"row": target}, device_id_type=MESH,
        )
        copy.start()
        end_copies.append(copy)
    total[0] = jnp.zeros((rows, rows), F32)
    total[4] = jnp.zeros((rows, rows), F32)
    for slot in range(3):
        total[1 + places[slot]] = panels[slot, :, :rows].T
    for index, place in ((0, 2 * (1 - odd)), (1, 2 * odd)):
        end_copies[index].wait_recv()
        for k in range(3):
            total[place + k] += arriving[index, k]
    for c in range(5):
        out_ref[:, c * rows:(c + 1) * rows] = total[c] * -2.0
    for copy in outer_copies + inner_copies + fwd_copies + end_copies:
        copy.wait_send()


def per_device(tau_count, row_count, integrals, occupied, virtual, tile_mask):
    rows, col_count, band_count, square = integrals.shape
    width = occupied.shape[-1]
    blocks = occupied.shape[0]
    n = lax.axis_index("row")
    odd = lax.rem(n, 2)
    tiles = integrals.transpose(1, 2, 0, 3).reshape(col_count * band_count, rows, square)

    around = (n - 1 + jnp.arange(3, dtype=jnp.int32)) % blocks
    occ = jnp.take(occupied, around, axis=0)
    vir = jnp.take(virtual, around, axis=0)
    flags = jnp.take(tile_mask, around, axis=0).reshape(3, 9)
    scale = flags.astype(BF16)

    own_w = jnp.stack([
        scale[1, 1:4, None, None] * occ[0, 2],
        scale[1, 3:6, None, None] * occ[1, 1],
        scale[1, 5:8, None, None] * occ[2, 0],
    ])
    keep_high = jnp.array([0, 1, 1], BF16)
    keep_low = jnp.array([1, 1, 0], BF16)
    right_w = jnp.stack([
        scale[2, 0:3, None, None] * occ[1, 1],
        (keep_high * scale[2, 2:5])[:, None, None] * occ[2, 0],
    ])
    left_w = jnp.stack([
        (keep_low * scale[0, 4:7])[:, None, None] * occ[0, 2],
        scale[0, 6:9, None, None] * occ[1, 1],
    ])
    inner_w = jnp.where(odd == 0, right_w, left_w)
    outer_w = jnp.where(odd == 0, left_w, right_w)
    small = jnp.swapaxes(jnp.concatenate([own_w, inner_w, outer_w]), 2, 3)
    eye = jnp.eye(2, dtype=BF16)
    weight = (small[:, :, None, :, None, :] * eye[None, None, :, None, :, None]).reshape(
        7, 3, 2 * width, 2 * width)

    zero = jnp.zeros((width, width), BF16)
    vmat = jnp.block([
        [vir[a, b - a + 1] if 0 <= b - a + 1 < 3 else zero for b in range(3)] for a in range(3)
    ])
    right_gate, left_gate = flags[2, 0:3], flags[0, 6:9]
    gates = jnp.stack([
        flags[1, 3:6],
        jnp.where(odd == 0, right_gate, left_gate),
        jnp.where(odd == 0, left_gate, right_gate),
    ]).astype(F32)

    vmem = pl.BlockSpec(memory_space=pltpu.VMEM)
    dma = pltpu.SemaphoreType.DMA
    return pl.pallas_call(
        functools.partial(kernel, tau_count, row_count, width),
        out_shape=jax.ShapeDtypeStruct((rows, 5 * rows), F32),
        in_specs=[
            pl.BlockSpec(memory_space=pl.ANY), vmem, vmem,
            pl.BlockSpec(memory_space=pltpu.SMEM),
        ],
        out_specs=vmem,
        scratch_shapes=[
            pltpu.VMEM((9, rows, square), BF16),
            pltpu.VMEM((2, NB_TILES, rows, square), BF16),
            pltpu.VMEM((3, square, rows), F32),
            pltpu.VMEM((3, square, rows), F32),
            pltpu.VMEM((3, square, 3 * rows), BF16),
            pltpu.VMEM((3, rows, 3 * rows), F32),
            pltpu.VMEM((2, 3, rows, rows), F32),
            pltpu.VMEM((2, 3, rows, rows), F32),
            pltpu.VMEM((5, rows, rows), F32),
            dma, dma((NB_TILES,)), dma((NB_TILES,)), dma((NB_TILES,)), dma((NB_TILES,)),
            dma((NB_TILES, max(1, tau_count - 1))), dma((NB_TILES, max(1, tau_count - 1))),
            dma((2,)), dma((2,)),
        ],
        compiler_params=pltpu.CompilerParams(
            collective_id=0, has_side_effects=True, vmem_limit_bytes=56 * 1024 * 1024),
    )(tiles, weight, vmat, gates)


def solution(mesh):
    in_specs = (
        P("row", None, None, None),
        P("tau", None, None, None),
        P("tau", None, None, None),
        P(),
    )
    out_specs = P(("tau", "row"), None)
    return jax.shard_map(
        functools.partial(per_device, mesh.shape["tau"], mesh.shape["row"]),
        mesh=mesh, in_specs=in_specs, out_specs=out_specs, check_vma=False,
    )
```

time: 196 us -> 142 us (0.72)
  Pallas kernels: 0 us -> 129 us
  starting transfers between devices: 73.2 us -> 0 us
  matrix products: 48.7 us -> 0 us
  waiting for transfers between devices: 29.1 us -> 0 us
  local copies, waits for them, and re-layouts: 25 us -> 7.92 us
  other arithmetic: 18.8 us -> 3.67 us
    pallas_call x0 -> x1, Pallas kernels: none -> 129 us  [per_device(): pl.pallas_call(functools.partial(kernel, tau_count, row_count, width), ou...]
    ppermute x6 -> x0, starting transfers between devices: 73.2 us -> none  [shifted(): return lax.ppermute(value, axis, pairs)]
    dot_general x39 -> x0, matrix products: 48.7 us -> none  [the longest x17 21.1 us: occupied_side(): jnp.einsum('puv,vl->pul', masked[:, inner, offset], occ_near[inner, secon...]
    ppermute x6 -> x0, waiting for transfers between devices: 29.1 us -> none  [shifted(): return lax.ppermute(value, axis, pairs)]
    mul x1 -> x8, local copies, waits for them, and re-layouts: 12.7 us -> 2.39 us  [the longest x4 2.11 us: per_device(): small[:, :, None, :, None, :] * eye[None, None, :, None, :, None]]
    squeeze x3 -> x1, local copies, waits for them, and re-layouts: 9.8 us -> 0.01 us  [per_device(): vir[a, b - a + 1]]
    mul x2 -> x5, other arithmetic: 8.76 us -> 1.93 us  [the longest x1 0.9 us: per_device(): small[:, :, None, :, None, :] * eye[None, None, :, None, :, None]]
    concatenate x1 -> x2, other arithmetic: 4.87 us -> 0.8 us  [the longest x1 0.74 us: per_device(): jnp.block([[vir[a, b - a + 1] if 0 <= b - a + 1 < 3 else zero for b in ra...]
  transfers between devices with their start and end apart: 6 -> 0, of which waited for: 5 -> 0; matrix products, arithmetic and copies ran while one was open for 24% -> 0% of each run, Pallas kernels for 0% -> 0%
where the time goes in v1:
time: 142 us; the launch traced here: 141 us
  Pallas kernels  129 us (91%)
  local copies, waits for them, and re-layouts  7.92 us (6%)
  other arithmetic  3.67 us (3%)
    pallas_call x1, Pallas kernels, per_device(): pl.pallas_call(functools.partial(kernel, tau_count, row_count, width), ou...  129 us

profile of v1, /device:TPU:0, one launch (start us, length us, event | category | flops | bytes accessed | tf_op | source)
XLA Modules:
  0.0 140.8 jit_solution(5602742068715835866)
XLA Ops:
  0.0 0.0 copy-start
  0.1 0.8 copy.11
  0.9 0.6 gather_fusion
  1.5 0.1 gather.10
  1.6 0.1 fusion.3
  1.7 0.1 fusion.4
  1.7 0.6 add_convert_fusion.gate_ref
  2.3 0.7 slice_bitcast_fusion.11
  3.1 0.1 mul.203
  3.2 0.1 mul.204
  3.3 0.0 copy-done
  3.3 0.6 gather_fusion.2
  3.9 1.7 %gather_fusion.1 = bf16[3,3,64,64]{3,2,1,0:T(8,128)(2,1)S(1)} fusion(bf16[16,3,64,64]{3,2,1,0:T(8,128)(2,1)} %param.9, s32[1024]{0:T(1024)S(1)} %get-tuple-element.37), kind=kCustom, calls=%fused_computation.clone | custom fusion | bytes 147468 | tf_op jit(solution)/shard_map/jit(_take)/gather | solution.py:209
  5.6 0.1 broadcast_select_fusion
  5.7 0.7 maximum_maximum_fusion.virt_ref
  6.5 0.1 copy.14
  6.6 0.1 copy.13
  6.7 0.1 copy.12
  6.8 0.1 broadcast_multiply_fusion.2
  6.9 0.1 broadcast_multiply_fusion.4
  7.0 0.1 broadcast_multiply_fusion.3
  7.1 0.1 select_dynamic-update-slice_fusion.1
  7.1 0.1 select_dynamic-update-slice_fusion
  7.2 1.2 mul.201
  8.4 0.7 mul.202
  9.1 0.9 broadcast_multiply_fusion.weight_ref
  10.0 129.1 %shard_map.64 = f32[128,640]{1,0:T(8,128)} custom-call(bf16[9,128,4096]{2,1,0:T(8,128)(2,1)} %bitcast.40, bf16[7,3,128,128]{3,2,1,0:T(8,128)(2,1)} %broadcast_multiply_fusion.weight_ref, bf16[192,192]{1,0:T(8,128)(2,1)} %maximum_maximum_fusion.virt_ref, f32[3,3]{1,0:T(4,128)} %add_convert_fusion.gate_ref), custom_call_target="tpu_custom_call" | custom-call | tf_op jit(solution)/shard_map/pallas_call | solution.py:249
  139.1 1.7 %copy.20 = f32[128,640]{1,0:T(8,128)} copy(f32[128,640]{1,0:T(8,128)} %shard_map.64) | data formatting | bytes 655360
  (8 shorter events, 0.1 us)
Async XLA Ops:
  0.0 3.3 %copy-start = (bf16[16,3,64,64]{3,2,1,0:T(8,128)(2,1)S(1)}, bf16[16,3,64,64]{3,2,1,0:T(8,128)(2,1)}, u32[]{:S(2)}) copy-start(bf16[16,3,64,64]{3,2,1,0:T(8,128)(2,1)} %param.10) | copy-start | bytes 1179652

commit v2 on v1

--- a/solution.py
+++ b/solution.py
@@ -93,7 +93,7 @@
                 prod[o, pl.ds(lane + 128, 128), :] = result[:, rows:]
             return carry
 
-        lax.fori_loop(0, square // 256, at, 0)
+        lax.fori_loop(0, square // 256, at, 0, unroll=4)
 
     def virtual(block):
         def at(step, carry):
@@ -109,7 +109,7 @@
                         m * width:(m + 1) * width, half * rows:(half + 1) * rows]
             return carry
 
-        lax.fori_loop(0, width // 2, at, 0)
+        lax.fori_loop(0, width // 2, at, 0, unroll=4)
 
         def rounded(step, carry):
             place = pl.ds(pl.multiple_of(step * 512, 512), 512)
@@ -117,7 +117,7 @@
                 virt[m, place, block * rows:(block + 1) * rows] = part[m, place, :].astype(BF16)
             return carry
 
-        lax.fori_loop(0, square // 512, rounded, 0)
+        lax.fori_loop(0, square // 512, rounded, 0, unroll=2)
 
     def panel(load, slot, low, high):
         result = None
@@ -129,7 +129,7 @@
                     preferred_element_type=F32)
 
             term = lax.fori_loop(
-                0, square // 512, at, jnp.zeros((rows, (high - low) * rows), F32))
+                0, square // 512, at, jnp.zeros((rows, (high - low) * rows), F32), unroll=4)
             term = term * gate_ref[slot, m]
             result = term if result is None else result + term
         panels[slot, :, low * rows:high * rows] = result

time: 142 us -> 117 us (0.82)
  Pallas kernels: 129 us -> 103 us
    pallas_call x1, Pallas kernels: 129 us -> 103 us  [per_device(): pl.pallas_call(functools.partial(kernel, tau_count, row_count, width), ou...]
where the time goes in v2:
time: 117 us; the launch traced here: 115 us
  Pallas kernels  103 us (88%)
  local copies, waits for them, and re-layouts  7.92 us (7%)
  other arithmetic  3.67 us (3%)
    pallas_call x1, Pallas kernels, per_device(): pl.pallas_call(functools.partial(kernel, tau_count, row_count, width), ou...  103 us
    unnamed x4, local copies, waits for them, and re-layouts  2.57 us

profile of v2, /device:TPU:0, one launch (start us, length us, event | category | flops | bytes accessed | tf_op | source)
XLA Modules:
  0.0 115.2 jit_solution(38376627948088687)
XLA Ops:
  0.0 0.0 copy-start
  0.1 0.8 copy.11
  0.9 0.6 gather_fusion
  1.5 0.1 gather.10
  1.6 0.1 fusion.3
  1.7 0.1 fusion.4
  1.7 0.6 add_convert_fusion.gate_ref
  2.3 0.7 slice_bitcast_fusion.11
  3.1 0.1 mul.203
  3.2 0.1 mul.204
  3.3 0.0 copy-done
  3.3 0.6 gather_fusion.2
  3.9 1.7 %gather_fusion.1 = bf16[3,3,64,64]{3,2,1,0:T(8,128)(2,1)S(1)} fusion(bf16[16,3,64,64]{3,2,1,0:T(8,128)(2,1)} %param.9, s32[1024]{0:T(1024)S(1)} %get-tuple-element.37), kind=kCustom, calls=%fused_computation.clone | custom fusion | bytes 147468 | tf_op jit(solution)/shard_map/jit(_take)/gather | solution.py:209
  5.6 0.1 broadcast_select_fusion
  5.7 0.7 maximum_maximum_fusion.virt_ref
  6.5 0.1 copy.14
  6.6 0.1 copy.13
  6.7 0.1 copy.12
  6.8 0.1 broadcast_multiply_fusion.2
  6.9 0.1 broadcast_multiply_fusion.4
  7.0 0.1 broadcast_multiply_fusion.3
  7.1 0.1 select_dynamic-update-slice_fusion.1
  7.1 0.1 select_dynamic-update-slice_fusion
  7.2 1.2 %mul.201 = bf16[7,3,2,64,2,64]{5,4,3,2,1,0:T(2,128)(2,1)S(1)} broadcast(bf16[7,3,64,64]{3,2,1,0:T(8,128)(2,1)S(1)} %bitcast.41), dimensions={0,1,3,5} | broadcast | bytes 860160 | tf_op jit(solution)/shard_map/mul | solution.py:233
  8.4 0.7 mul.202
  9.1 0.9 broadcast_multiply_fusion.weight_ref
  10.0 103.5 %shard_map.64 = f32[128,640]{1,0:T(8,128)} custom-call(bf16[9,128,4096]{2,1,0:T(8,128)(2,1)} %bitcast.40, bf16[7,3,128,128]{3,2,1,0:T(8,128)(2,1)} %broadcast_multiply_fusion.weight_ref, bf16[192,192]{1,0:T(8,128)(2,1)} %maximum_maximum_fusion.virt_ref, f32[3,3]{1,0:T(4,128)} %add_convert_fusion.gate_ref), custom_call_target="tpu_custom_call" | custom-call | tf_op jit(solution)/shard_map/pallas_call | solution.py:249
  113.5 1.7 %copy.20 = f32[128,640]{1,0:T(8,128)} copy(f32[128,640]{1,0:T(8,128)} %shard_map.64) | data formatting | bytes 655360
  (8 shorter events, 0.1 us)
Async XLA Ops:
  0.0 3.3 %copy-start = (bf16[16,3,64,64]{3,2,1,0:T(8,128)(2,1)S(1)}, bf16[16,3,64,64]{3,2,1,0:T(8,128)(2,1)}, u32[]{:S(2)}) copy-start(bf16[16,3,64,64]{3,2,1,0:T(8,128)(2,1)} %param.10) | copy-start | bytes 1179652

commit v3 on v2

--- a/solution.py
+++ b/solution.py
@@ -11,14 +11,15 @@
 BF16 = jnp.bfloat16
 MESH = pl.DeviceIdType.MESH
 NB_TILES = 5
+ORDER = (0, 2, 1, 3, 4)
 OWN_TERMS = (((0, 1), (1, 3)), ((0, 2), (1, 4), (2, 6)), ((1, 5), (2, 7)))
 
 
 def kernel(
     tau_count, row_count, width,
-    tiles_ref, weight_ref, virt_ref, gate_ref,
+    tiles_ref, occ_ref, vir_ref, mask_ref,
     out_ref,
-    own, near, prod, part, virt, panels, sending, arriving, total,
+    weight_ref, virt_ref, own, near, prod, part, virt, panels, sending, arriving, total,
     own_sem, inner_send, inner_recv, outer_send, outer_recv, fwd_send, fwd_recv, end_send, end_recv,
 ):
     rows = own.shape[1]
@@ -40,8 +41,8 @@
         )
     pl.semaphore_wait(barrier, tau_count + 1)
 
-    outer_copies = []
-    for t in range(NB_TILES):
+    outer_copies = {}
+    for t in ORDER:
         copy = pltpu.make_async_remote_copy(
             src_ref=tiles_ref.at[4 * odd + t, pl.ds(first, share)],
             dst_ref=near.at[1, t, pl.ds(first, share)],
@@ -49,7 +50,7 @@
             device_id={"row": outer}, device_id_type=MESH,
         )
         copy.start()
-        outer_copies.append(copy)
+        outer_copies[t] = copy
     own_copy = pltpu.make_async_copy(tiles_ref, own, own_sem)
     own_copy.start()
     inner_copies = []
@@ -63,7 +64,7 @@
         copy.start()
         inner_copies.append(copy)
 
-    fwd_copies = []
+    fwd_copies = {t: [] for t in ORDER}
 
     def forward(t):
         outer_copies[t].wait_recv()
@@ -75,12 +76,57 @@
                 device_id={"tau": lax.rem(tau + step, tau_count)}, device_id_type=MESH,
             )
             copy.start()
-            fwd_copies.append(copy)
-
-    def products(load, base, terms):
+            fwd_copies[t].append(copy)
+
+    left = lax.rem(me - 1 + row_count, row_count)
+    right = lax.rem(me + 1, row_count)
+    inner_kind = (1 - odd).astype(F32)
+    outer_kind = odd.astype(F32)
+
+    def flag(block, tile):
+        return mask_ref[block, tile // 3, tile % 3].astype(F32)
+
+    def setup():
+        def spread(block):
+            turned = block.T
+            blank = jnp.zeros((width, width), F32)
+            return jnp.concatenate([
+                jnp.concatenate([turned, blank], axis=1),
+                jnp.concatenate([blank, turned], axis=1),
+            ], axis=0)
+
+        before = spread(occ_ref[left, 2].astype(F32))
+        middle = spread(occ_ref[me, 1].astype(F32))
+        after = spread(occ_ref[right, 0].astype(F32))
+        for o in range(3):
+            for k, (matrix, tile) in enumerate(((before, 1 + o), (middle, 3 + o), (after, 5 + o))):
+                weight_ref[k, o] = (matrix * flag(me, tile)).astype(BF16)
+            for base, kind in ((3, inner_kind), (5, outer_kind)):
+                other = 1.0 - kind
+                first_right = kind * flag(right, o)
+                second_right = kind * flag(right, 2 + o) if o > 0 else 0.0
+                first_left = other * flag(left, 4 + o) if o < 2 else 0.0
+                second_left = other * flag(left, 6 + o)
+                weight_ref[base, o] = (middle * first_right + before * first_left).astype(BF16)
+                weight_ref[base + 1, o] = (after * second_right + middle * second_left).astype(BF16)
+        owners = (left, me, right)
+        blank = jnp.zeros((width, width), F32)
+        for a in range(3):
+            virt_ref[a * width:(a + 1) * width, :] = jnp.concatenate([
+                vir_ref[owners[a], b - a + 1].astype(F32) if 0 <= b - a + 1 < 3 else blank
+                for b in range(3)
+            ], axis=1).astype(BF16)
+
+    def gate(slot, m):
+        if slot == 0:
+            return flag(me, 3 + m)
+        kind = inner_kind if slot == 1 else outer_kind
+        return kind * flag(right, m) + (1.0 - kind) * flag(left, 6 + m)
+
+    def products(load, base, terms, bands=(0, 1, 2)):
         def at(step, carry):
             lane = pl.multiple_of(step * 256, 256)
-            for o in range(3):
+            for o in bands:
                 halves = []
                 for half in range(2):
                     halves.append(jnp.concatenate(
@@ -130,7 +176,7 @@
 
             term = lax.fori_loop(
                 0, square // 512, at, jnp.zeros((rows, (high - low) * rows), F32), unroll=4)
-            term = term * gate_ref[slot, m]
+            term = term * gate(slot, m)
             result = term if result is None else result + term
         panels[slot, :, low * rows:high * rows] = result
 
@@ -148,6 +194,11 @@
 
     near_terms = tuple(((0, o), (1, 2 + o)) for o in range(3))
 
+    def arrived(t):
+        for copy in fwd_copies[t]:
+            copy.wait_recv()
+
+    setup()
     own_copy.wait()
     products(own_load, 0, OWN_TERMS)
     virtual(0)
@@ -156,93 +207,66 @@
     for copy in inner_copies:
         copy.wait_recv()
     products(near_load(0), 3, near_terms)
-    forward(1)
+    forward(2)
     virtual(1)
     panel(near_partner(0, 2 * odd), 1, 0, 2)
     panel(own_partner, 0, 1, 2)
-    for t in range(2, NB_TILES):
-        forward(t)
-    for copy in fwd_copies:
-        copy.wait_recv()
-    products(near_load(1), 5, near_terms)
+    forward(1)
+    arrived(0)
+    arrived(2)
+    products(near_load(1), 5, near_terms, (0,))
+    forward(3)
+    arrived(1)
+    arrived(3)
+    products(near_load(1), 5, near_terms, (1,))
+    forward(4)
+    arrived(4)
+    products(near_load(1), 5, near_terms, (2,))
     virtual(2)
-    panel(near_partner(1, 2 * (1 - odd)), 2, 0, 3)
-    panel(own_partner, 0, 2, 3)
-    panel(near_partner(0, 2 * odd), 1, 2, 3)
 
     places = (1, 2 * (1 - odd), 2 * odd)
-    for block in (1, 2):
-        for slot in range(3):
-            sending[block - 1, places[slot]] = panels[slot, :, block * rows:(block + 1) * rows].T
     end_copies = []
-    for block, target in ((1, inner), (2, outer)):
+
+    def finish(block, slot, target):
+        sending[block - 1, slot] = panels[slot, :, block * rows:(block + 1) * rows].T
         copy = pltpu.make_async_remote_copy(
-            src_ref=sending.at[block - 1], dst_ref=arriving.at[block - 1],
-            send_sem=end_send.at[block - 1], recv_sem=end_recv.at[block - 1],
+            src_ref=sending.at[block - 1, slot], dst_ref=arriving.at[block - 1, places[slot]],
+            send_sem=end_send.at[block - 1, slot], recv_sem=end_recv.at[block - 1, slot],
             device_id={"row": target}, device_id_type=MESH,
         )
         copy.start()
         end_copies.append(copy)
+
+    panel(own_partner, 0, 2, 3)
+    finish(2, 0, outer)
+    panel(near_partner(0, 2 * odd), 1, 2, 3)
+    finish(2, 1, outer)
+    panel(near_partner(1, 2 * (1 - odd)), 2, 0, 3)
+    finish(2, 2, outer)
+    for slot in range(3):
+        finish(1, slot, inner)
     total[0] = jnp.zeros((rows, rows), F32)
     total[4] = jnp.zeros((rows, rows), F32)
     for slot in range(3):
         total[1 + places[slot]] = panels[slot, :, :rows].T
+    for copy in end_copies:
+        copy.wait_recv()
     for index, place in ((0, 2 * (1 - odd)), (1, 2 * odd)):
-        end_copies[index].wait_recv()
         for k in range(3):
             total[place + k] += arriving[index, k]
     for c in range(5):
         out_ref[:, c * rows:(c + 1) * rows] = total[c] * -2.0
-    for copy in outer_copies + inner_copies + fwd_copies + end_copies:
+    for copy in list(outer_copies.values()) + inner_copies + end_copies:
         copy.wait_send()
+    for group in fwd_copies.values():
+        for copy in group:
+            copy.wait_send()
 
 
 def per_device(tau_count, row_count, integrals, occupied, virtual, tile_mask):
     rows, col_count, band_count, square = integrals.shape
     width = occupied.shape[-1]
-    blocks = occupied.shape[0]
-    n = lax.axis_index("row")
-    odd = lax.rem(n, 2)
     tiles = integrals.transpose(1, 2, 0, 3).reshape(col_count * band_count, rows, square)
-
-    around = (n - 1 + jnp.arange(3, dtype=jnp.int32)) % blocks
-    occ = jnp.take(occupied, around, axis=0)
-    vir = jnp.take(virtual, around, axis=0)
-    flags = jnp.take(tile_mask, around, axis=0).reshape(3, 9)
-    scale = flags.astype(BF16)
-
-    own_w = jnp.stack([
-        scale[1, 1:4, None, None] * occ[0, 2],
-        scale[1, 3:6, None, None] * occ[1, 1],
-        scale[1, 5:8, None, None] * occ[2, 0],
-    ])
-    keep_high = jnp.array([0, 1, 1], BF16)
-    keep_low = jnp.array([1, 1, 0], BF16)
-    right_w = jnp.stack([
-        scale[2, 0:3, None, None] * occ[1, 1],
-        (keep_high * scale[2, 2:5])[:, None, None] * occ[2, 0],
-    ])
-    left_w = jnp.stack([
-        (keep_low * scale[0, 4:7])[:, None, None] * occ[0, 2],
-        scale[0, 6:9, None, None] * occ[1, 1],
-    ])
-    inner_w = jnp.where(odd == 0, right_w, left_w)
-    outer_w = jnp.where(odd == 0, left_w, right_w)
-    small = jnp.swapaxes(jnp.concatenate([own_w, inner_w, outer_w]), 2, 3)
-    eye = jnp.eye(2, dtype=BF16)
-    weight = (small[:, :, None, :, None, :] * eye[None, None, :, None, :, None]).reshape(
-        7, 3, 2 * width, 2 * width)
-
-    zero = jnp.zeros((width, width), BF16)
-    vmat = jnp.block([
-        [vir[a, b - a + 1] if 0 <= b - a + 1 < 3 else zero for b in range(3)] for a in range(3)
-    ])
-    right_gate, left_gate = flags[2, 0:3], flags[0, 6:9]
-    gates = jnp.stack([
-        flags[1, 3:6],
-        jnp.where(odd == 0, right_gate, left_gate),
-        jnp.where(odd == 0, left_gate, right_gate),
-    ]).astype(F32)
 
     vmem = pl.BlockSpec(memory_space=pltpu.VMEM)
     dma = pltpu.SemaphoreType.DMA
@@ -255,6 +279,8 @@
         ],
         out_specs=vmem,
         scratch_shapes=[
+            pltpu.VMEM((7, 3, 2 * width, 2 * width), BF16),
+            pltpu.VMEM((3 * width, 3 * width), BF16),
             pltpu.VMEM((9, rows, square), BF16),
             pltpu.VMEM((2, NB_TILES, rows, square), BF16),
             pltpu.VMEM((3, square, rows), F32),
@@ -266,11 +292,11 @@
             pltpu.VMEM((5, rows, rows), F32),
             dma, dma((NB_TILES,)), dma((NB_TILES,)), dma((NB_TILES,)), dma((NB_TILES,)),
             dma((NB_TILES, max(1, tau_count - 1))), dma((NB_TILES, max(1, tau_count - 1))),
-            dma((2,)), dma((2,)),
+            dma((2, 3)), dma((2, 3)),
         ],
         compiler_params=pltpu.CompilerParams(
             collective_id=0, has_side_effects=True, vmem_limit_bytes=56 * 1024 * 1024),
-    )(tiles, weight, vmat, gates)
+    )(tiles, occupied, virtual, tile_mask)
 
 
 def solution(mesh):

time: 117 us -> 108 us (0.923); the launches traced: 115 us -> 108 us
  local copies, waits for them, and re-layouts: 7.92 us -> 3.12 us
  other arithmetic: 3.67 us -> 0 us
  Pallas kernels: 103 us -> 105 us
    gather x4 -> x0, local copies, waits for them, and re-layouts: 2.94 us -> none  [the longest x1 1.71 us: per_device(): occ = jnp.take(occupied, around, axis=0)]
    mul x8 -> x0, local copies, waits for them, and re-layouts: 2.39 us -> none  [the longest x4 2.11 us: per_device(): small[:, :, None, :, None, :] * eye[None, None, :, None, :, None]]
    mul x5 -> x0, other arithmetic: 1.93 us -> none  [the longest x1 0.9 us: per_device(): small[:, :, None, :, None, :] * eye[None, None, :, None, :, None]]
    pallas_call x1, Pallas kernels: 103 us -> 105 us  [per_device(): pl.pallas_call(functools.partial(kernel, tau_count, row_count, width), ou...]
    unnamed x4 -> x2, local copies, waits for them, and re-layouts: 2.57 us -> 3.12 us
where the time goes in v3:
time: 108 us
  Pallas kernels  105 us (97%)
  local copies, waits for them, and re-layouts  3.12 us (3%)
    pallas_call x1, Pallas kernels, per_device(): pl.pallas_call(functools.partial(kernel, tau_count, row_count, width), ou...  105 us
    unnamed x2, local copies, waits for them, and re-layouts  3.12 us

profile of v3, /device:TPU:0, one launch (start us, length us, event | category | flops | bytes accessed | tf_op | source)
XLA Modules:
  0.0 108.2 jit_solution(8722409490060114206)
XLA Ops:
  0.0 1.4 %copy.5.mask_ref = s32[16,3,3]{2,1,0:T(4,128)} copy(s32[16,3,3]{0,2,1:T(4,128)} %param.7) | data formatting | bytes 1152 | tf_op args[3]
  1.4 105.1 %shard_map.46 = f32[128,640]{1,0:T(8,128)} custom-call(bf16[9,128,4096]{2,1,0:T(8,128)(2,1)} %bitcast.3, bf16[16,3,64,64]{3,2,1,0:T(8,128)(2,1)} %occ_ref.1, bf16[16,3,64,64]{3,2,1,0:T(8,128)(2,1)} %vir_ref.1, s32[16,3,3]{2,1,0:T(4,128)} %copy.5.mask_ref), custom_call_target="tpu_custom_call" | custom-call | tf_op jit(solution)/shard_map/pallas_call | solution.py:273
  106.5 1.7 %copy.7 = f32[128,640]{1,0:T(8,128)} copy(f32[128,640]{1,0:T(8,128)} %shard_map.46) | data formatting | bytes 655360

commit v4 on v3

--- a/solution.py
+++ b/solution.py
@@ -24,6 +24,7 @@
 ):
     rows = own.shape[1]
     square = own.shape[2]
+    pitch = prod.shape[1] // width
     tau = lax.axis_index("tau")
     me = lax.axis_index("row")
     odd = lax.rem(me, 2)
@@ -135,8 +136,10 @@
                 result = lax.dot_general(
                     weight, jnp.concatenate(halves, axis=0), (((1,), (1,)), ((), ())),
                     preferred_element_type=F32)
-                prod[o, pl.ds(lane, 128), :] = result[:, :rows]
-                prod[o, pl.ds(lane + 128, 128), :] = result[:, rows:]
+                for q in range(4):
+                    place = pl.ds(pl.multiple_of((4 * step + q) * pitch, 8), width)
+                    prod[o, place, :] = result[
+                        (q % 2) * width:(q % 2 + 1) * width, (q // 2) * rows:(q // 2 + 1) * rows]
             return carry
 
         lax.fori_loop(0, square // 256, at, 0, unroll=4)
@@ -146,12 +149,12 @@
             columns = []
             for half in range(2):
                 columns.append(jnp.concatenate(
-                    [prod[m, pl.ds(2 * step + half, width, stride=width), :] for m in range(3)], axis=0))
+                    [prod[m, pl.ds(2 * step + half, width, stride=pitch), :] for m in range(3)], axis=0))
             right = jnp.concatenate(columns, axis=1).astype(BF16)
             result = jnp.dot(virt_ref[...], right, preferred_element_type=F32)
             for half in range(2):
                 for m in range(3):
-                    part[m, pl.ds(2 * step + half, width, stride=width), :] = result[
+                    part[m, pl.ds(2 * step + half, width, stride=pitch), :] = result[
                         m * width:(m + 1) * width, half * rows:(half + 1) * rows]
             return carry
 
@@ -160,14 +163,17 @@
         def rounded(step, carry):
             place = pl.ds(pl.multiple_of(step * 512, 512), 512)
             for m in range(3):
-                virt[m, place, block * rows:(block + 1) * rows] = part[m, place, :].astype(BF16)
+                virt[m, place, block * rows:(block + 1) * rows] = jnp.concatenate([
+                    part[m, pl.ds(pl.multiple_of((8 * step + q) * pitch, 8), width), :]
+                    for q in range(8)
+                ], axis=0).astype(BF16)
             return carry
 
         lax.fori_loop(0, square // 512, rounded, 0, unroll=2)
 
-    def panel(load, slot, low, high):
-        result = None
-        for m in range(3):
+    def panel(load, slot, low, high, bands=(0, 1, 2), more=False):
+        result = panels[slot, :, low * rows:high * rows] if more else None
+        for m in bands:
             def at(step, carry, m=m):
                 place = pl.ds(pl.multiple_of(step * 512, 512), 512)
                 return carry + jnp.dot(
@@ -217,9 +223,10 @@
     products(near_load(1), 5, near_terms, (0,))
     forward(3)
     arrived(1)
+    forward(4)
     arrived(3)
     products(near_load(1), 5, near_terms, (1,))
-    forward(4)
+    panel(near_partner(1, 2 * (1 - odd)), 2, 0, 2, (0, 1))
     arrived(4)
     products(near_load(1), 5, near_terms, (2,))
     virtual(2)
@@ -241,8 +248,9 @@
     finish(2, 0, outer)
     panel(near_partner(0, 2 * odd), 1, 2, 3)
     finish(2, 1, outer)
-    panel(near_partner(1, 2 * (1 - odd)), 2, 0, 3)
+    panel(near_partner(1, 2 * (1 - odd)), 2, 2, 3)
     finish(2, 2, outer)
+    panel(near_partner(1, 2 * (1 - odd)), 2, 0, 2, (2,), True)
     for slot in range(3):
         finish(1, slot, inner)
     total[0] = jnp.zeros((rows, rows), F32)
@@ -283,8 +291,8 @@
             pltpu.VMEM((3 * width, 3 * width), BF16),
             pltpu.VMEM((9, rows, square), BF16),
             pltpu.VMEM((2, NB_TILES, rows, square), BF16),
-            pltpu.VMEM((3, square, rows), F32),
-            pltpu.VMEM((3, square, rows), F32),
+            pltpu.VMEM((3, square + 8 * width, rows), F32),
+            pltpu.VMEM((3, square + 8 * width, rows), F32),
             pltpu.VMEM((3, square, 3 * rows), BF16),
             pltpu.VMEM((3, rows, 3 * rows), F32),
             pltpu.VMEM((2, 3, rows, rows), F32),

time: 108 us -> 91.3 us (0.85)
  Pallas kernels: 105 us -> 88 us
    pallas_call x1, Pallas kernels: 105 us -> 88 us  [per_device(): pl.pallas_call(functools.partial(kernel, tau_count, row_count, width), ou...]
where the time goes in v4:
time: 91.3 us; the launch traced here: 91.1 us
  Pallas kernels  88 us (96%)
  local copies, waits for them, and re-layouts  3.12 us (3%)
    pallas_call x1, Pallas kernels, per_device(): pl.pallas_call(functools.partial(kernel, tau_count, row_count, width), ou...  88 us
    unnamed x2, local copies, waits for them, and re-layouts  3.12 us

profile of v4, /device:TPU:0, one launch (start us, length us, event | category | flops | bytes accessed | tf_op | source)
XLA Modules:
  0.0 91.1 jit_solution(3698957263524662896)
XLA Ops:
  0.0 1.4 %copy.5.mask_ref = s32[16,3,3]{2,1,0:T(4,128)} copy(s32[16,3,3]{0,2,1:T(4,128)} %param.7) | data formatting | bytes 1152 | tf_op args[3]
  1.4 88.0 %shard_map.46 = f32[128,640]{1,0:T(8,128)} custom-call(bf16[9,128,4096]{2,1,0:T(8,128)(2,1)} %bitcast.3, bf16[16,3,64,64]{3,2,1,0:T(8,128)(2,1)} %occ_ref.1, bf16[16,3,64,64]{3,2,1,0:T(8,128)(2,1)} %vir_ref.1, s32[16,3,3]{2,1,0:T(4,128)} %copy.5.mask_ref), custom_call_target="tpu_custom_call" | custom-call | tf_op jit(solution)/shard_map/pallas_call | solution.py:281
  89.4 1.7 %copy.7 = f32[128,640]{1,0:T(8,128)} copy(f32[128,640]{1,0:T(8,128)} %shard_map.46) | data formatting | bytes 655360

commit v5 on v4

--- a/solution.py
+++ b/solution.py
@@ -158,7 +158,7 @@
                         m * width:(m + 1) * width, half * rows:(half + 1) * rows]
             return carry
 
-        lax.fori_loop(0, width // 2, at, 0, unroll=4)
+        lax.fori_loop(0, width // 2, at, 0, unroll=8)
 
         def rounded(step, carry):
             place = pl.ds(pl.multiple_of(step * 512, 512), 512)
@@ -181,7 +181,7 @@
                     preferred_element_type=F32)
 
             term = lax.fori_loop(
-                0, square // 512, at, jnp.zeros((rows, (high - low) * rows), F32), unroll=4)
+                0, square // 512, at, jnp.zeros((rows, (high - low) * rows), F32), unroll=8)
             term = term * gate(slot, m)
             result = term if result is None else result + term
         panels[slot, :, low * rows:high * rows] = result
@@ -203,6 +203,19 @@
     def arrived(t):
         for copy in fwd_copies[t]:
             copy.wait_recv()
+
+    places = (1, 2 * (1 - odd), 2 * odd)
+    end_copies = []
+
+    def finish(block, slot, target):
+        sending[block - 1, slot] = panels[slot, :, block * rows:(block + 1) * rows].T
+        copy = pltpu.make_async_remote_copy(
+            src_ref=sending.at[block - 1, slot], dst_ref=arriving.at[block - 1, places[slot]],
+            send_sem=end_send.at[block - 1, slot], recv_sem=end_recv.at[block - 1, slot],
+            device_id={"row": target}, device_id_type=MESH,
+        )
+        copy.start()
+        end_copies.append(copy)
 
     setup()
     own_copy.wait()
@@ -227,22 +240,14 @@
     arrived(3)
     products(near_load(1), 5, near_terms, (1,))
     panel(near_partner(1, 2 * (1 - odd)), 2, 0, 2, (0, 1))
+    total[0] = jnp.zeros((rows, rows), F32)
+    total[4] = jnp.zeros((rows, rows), F32)
+    for slot in range(2):
+        finish(1, slot, inner)
+        total[1 + places[slot]] = panels[slot, :, :rows].T
     arrived(4)
     products(near_load(1), 5, near_terms, (2,))
     virtual(2)
-
-    places = (1, 2 * (1 - odd), 2 * odd)
-    end_copies = []
-
-    def finish(block, slot, target):
-        sending[block - 1, slot] = panels[slot, :, block * rows:(block + 1) * rows].T
-        copy = pltpu.make_async_remote_copy(
-            src_ref=sending.at[block - 1, slot], dst_ref=arriving.at[block - 1, places[slot]],
-            send_sem=end_send.at[block - 1, slot], recv_sem=end_recv.at[block - 1, slot],
-            device_id={"row": target}, device_id_type=MESH,
-        )
-        copy.start()
-        end_copies.append(copy)
 
     panel(own_partner, 0, 2, 3)
     finish(2, 0, outer)
@@ -251,12 +256,8 @@
     panel(near_partner(1, 2 * (1 - odd)), 2, 2, 3)
     finish(2, 2, outer)
     panel(near_partner(1, 2 * (1 - odd)), 2, 0, 2, (2,), True)
-    for slot in range(3):
-        finish(1, slot, inner)
-    total[0] = jnp.zeros((rows, rows), F32)
-    total[4] = jnp.zeros((rows, rows), F32)
-    for slot in range(3):
-        total[1 + places[slot]] = panels[slot, :, :rows].T
+    finish(1, 2, inner)
+    total[1 + places[2]] = panels[2, :, :rows].T
     for copy in end_copies:
         copy.wait_recv()
     for index, place in ((0, 2 * (1 - odd)), (1, 2 * odd)):

time: 91.3 us -> 88.2 us (0.966)
  Pallas kernels: 88 us -> 84.9 us
    pallas_call x1, Pallas kernels: 88 us -> 84.9 us  [per_device(): pl.pallas_call(functools.partial(kernel, tau_count, row_count, width), ou...]
where the time goes in v5:
time: 88.2 us; the launch traced here: 88 us
  Pallas kernels  84.9 us (96%)
  local copies, waits for them, and re-layouts  3.12 us (4%)
    pallas_call x1, Pallas kernels, per_device(): pl.pallas_call(functools.partial(kernel, tau_count, row_count, width), ou...  84.9 us
    unnamed x2, local copies, waits for them, and re-layouts  3.12 us

profile of v5, /device:TPU:0, one launch (start us, length us, event | category | flops | bytes accessed | tf_op | source)
XLA Modules:
  0.0 88.0 jit_solution(17704449886147683710)
XLA Ops:
  0.0 1.4 %copy.5.mask_ref = s32[16,3,3]{2,1,0:T(4,128)} copy(s32[16,3,3]{0,2,1:T(4,128)} %param.7) | data formatting | bytes 1152 | tf_op args[3]
  1.4 84.9 %shard_map.46 = f32[128,640]{1,0:T(8,128)} custom-call(bf16[9,128,4096]{2,1,0:T(8,128)(2,1)} %bitcast.3, bf16[16,3,64,64]{3,2,1,0:T(8,128)(2,1)} %occ_ref.1, bf16[16,3,64,64]{3,2,1,0:T(8,128)(2,1)} %vir_ref.1, s32[16,3,3]{2,1,0:T(4,128)} %copy.5.mask_ref), custom_call_target="tpu_custom_call" | custom-call | tf_op jit(solution)/shard_map/pallas_call | solution.py:282
  86.3 1.7 %copy.7 = f32[128,640]{1,0:T(8,128)} copy(f32[128,640]{1,0:T(8,128)} %shard_map.46) | data formatting | bytes 655360
